TPU v7x, 32 devices: a whole 2x2x4 slice. The times are simulated.
32 devices in a mesh: group: 4 (over y, x), dom: 8 (over z, core).
Axes of the slice: x: 2, y: 2, z: 4, core: 2. Of those that a mesh axis runs over, the one named last changes fastest.
Arguments:
- density: float32 [64, 16384], P(None, ('group', 'dom')), may hold values from 0.8 to 1.2
- momentum: float32 [3, 64, 16384], P(None, None, ('group', 'dom')), may hold values from -0.5 to 0.5
- energy: float32 [64, 16384], P(None, ('group', 'dom')), may hold values from 2.5 to 3.5
- face_link: int32 [4, 8, 3072], P('group', 'dom'), may hold values from 0 to 3455, as said below
- owner_rank: int32 [4096, 1], P(('group', 'dom')), may hold values from 0 to 7; in each aligned block of 128 rows (0 to 127, 128 to 255, ...) at most 32 rows name the same one
- owner_element: int32 [4, 4096], P(None, ('group', 'dom')), may hold values from 0 to 511
- point_offset: float32 [3, 4, 4096], P(None, None, ('group', 'dom')), may hold values from -1.5 to 1.5
- point_force: float32 [3, 4096], P(None, ('group', 'dom')), may hold values from -4 to 4
Outputs:
- new_density: float32 [64, 16384], P(None, ('group', 'dom'))
- new_momentum: float32 [3, 64, 16384], P(None, None, ('group', 'dom'))
- new_energy: float32 [64, 16384], P(None, ('group', 'dom'))
- tendency: float32 [5, 64, 16384], P(None, None, ('group', 'dom'))
Inputs may be any that keep to these rules, and one draw needn't show every extreme that they name: `face_link`: on each device the values are all different; every value from 3072 up appears exactly once, and a value v below 3072 on face f means that face v has the value f: faces within a device are paired. `owner_rank`: in the 128 rows of one device no value appears more than 32 times, and in every draw some device names some value exactly 32 times.
All inputs are finite; a program needn't handle non-finite values.
Results may differ from a plain program's by a relative error of at most 0.0003.
Values sent between devices are 32-bit elements; how exact they have to be, the bound alone decides.
A program may use at most 64 MiB of HBM per device.

v0:
```python
import functools
import math

import jax
import jax.numpy as jnp
import numpy as np
from jax import lax
from jax.experimental import pallas as pl
from jax.experimental.pallas import tpu as pltpu
from jax.sharding import PartitionSpec as P

CAP = 32
TIME_STEP = 0.005
SPREAD_WIDTH = 0.5
LIFT_FACTOR = 6.0
HEAT_RATIO = 1.4
LANES = 128
NODES = 64
ROWS = 80
MESH = pl.DeviceIdType.MESH
F32 = jnp.float32
BF16 = jnp.bfloat16


def basis_tables():
    nodes = np.array([-1.0, -math.sqrt(0.2), math.sqrt(0.2), 1.0])
    weights = np.array(
        [1.0 / np.prod([nodes[a] - nodes[c] for c in range(4) if c != a]) for a in range(4)]
    )
    deriv = np.zeros((4, 4))
    for a in range(4):
        for b in range(4):
            if a != b:
                deriv[a, b] = weights[b] / weights[a] / (nodes[a] - nodes[b])
        deriv[a, a] = -np.sum(deriv[a])
    vander = np.stack(
        [np.ones(4), nodes, 1.5 * nodes**2 - 0.5, 2.5 * nodes**3 - 1.5 * nodes], axis=1
    )
    one_dim = vander * np.array([1.0, 1.0, 1.0, 0.75])[None, :] @ np.linalg.inv(vander)
    eye = np.eye(4)
    dcat = np.concatenate(
        [
            np.kron(eye, np.kron(eye, deriv)),
            np.kron(eye, np.kron(deriv, eye)),
            np.kron(deriv, np.kron(eye, eye)),
        ],
        axis=1,
    )
    filt = np.kron(one_dim, np.kron(one_dim, one_dim))
    return nodes, dcat, filt


def split_table(table):
    table = np.asarray(table, np.float32)
    high = table.astype(BF16)
    low = (table - high.astype(np.float32)).astype(BF16)
    top = np.concatenate([high, high], axis=1)
    bottom = np.concatenate([low, np.zeros_like(low)], axis=1)
    return np.concatenate([top, bottom], axis=0)


def split2(x):
    high = x.astype(BF16)
    return high, (x - high.astype(F32)).astype(BF16)


def split3(x):
    high = x.astype(BF16)
    rest = x - high.astype(F32)
    middle = rest.astype(BF16)
    return high, middle, (rest - middle.astype(F32)).astype(BF16)


def dot_nt(a, b):
    return lax.dot_general(a, b, (((1,), (1,)), ((), ())), preferred_element_type=F32)


def pick_lanes(x, index):
    return jnp.take_along_axis(x, index, axis=1, mode="promise_in_bounds")


def state_of(rows):
    inverse = 1.0 / rows[0]
    vel = [rows[1 + c] * inverse for c in range(3)]
    press = (HEAT_RATIO - 1.0) * (
        rows[4] - 0.5 * (rows[1] * vel[0] + rows[2] * vel[1] + rows[3] * vel[2])
    )
    return inverse, vel, press


def flux_of(rows, vel, press, d):
    along = vel[d]
    out = [
        rows[1 + d],
        rows[1] * along,
        rows[2] * along,
        rows[3] * along,
        (rows[4] + press) * along,
    ]
    out[1 + d] = out[1 + d] + press
    return out


def kernel(
    nd, ng, nodes,
    den, mom, ene, link, rank, elem, off, force, dmat, fmat,
    o_den, o_mom, o_ene, o_tend,
    q, q1, td, tr, nb, t3, oh, lk, fx, xf, ex, src, ohe, ct,
    s1, r1, s2, r2, rs, rr, send_sem, recv_sem, rim_send_sem, rim_recv_sem,
):
    width = den.shape[1]
    cols = width // LANES
    blocks = 6 * cols
    shared = nd * (width // 32)
    shared_blocks = shared // LANES
    extra = shared_blocks + 2
    me = lax.axis_index("dom")
    group = lax.axis_index("group")
    up, down = lax.rem(group + 1, ng), lax.rem(group + ng - 1, ng)

    barrier = pltpu.get_barrier_semaphore()
    for d in range(1, nd):
        pl.semaphore_signal(
            barrier, inc=1, device_id={"dom": lax.rem(me + d, nd)}, device_id_type=MESH
        )
    for target in (up, down):
        pl.semaphore_signal(barrier, inc=1, device_id={"group": target}, device_id_type=MESH)

    def at(v, c):
        return (v * cols + c) * NODES

    for c in range(cols):
        lanes = slice(c * LANES, (c + 1) * LANES)
        q[at(0, c) : at(0, c) + NODES, :] = den[:, lanes]
        for v in range(3):
            q[at(1 + v, c) : at(1 + v, c) + NODES, :] = mom[v, :, lanes]
        q[at(4, c) : at(4, c) + NODES, :] = ene[:, lanes]

    row_ids = lax.broadcasted_iota(jnp.int32, (extra * LANES, LANES), 0) + 6 * width
    for b in range(blocks):
        part = link[0:1, b * LANES : (b + 1) * LANES]
        lk[b] = jnp.broadcast_to(part, (8, LANES))
        oh[:, b * LANES : (b + 1) * LANES] = jnp.where(row_ids == part, 1.0, 0.0).astype(BF16)

    def fill_traces(ref):
        for c in range(cols):
            for v in range(5):
                base = at(v, c)
                for t in range(6):
                    dst = (t * cols + c) * ROWS + v * 16
                    if t < 2:
                        tr[dst : dst + 16, :] = ref[pl.ds(base + 3 * t, 16, 4), :]
                    elif t < 4:
                        for k in range(4):
                            first = base + 16 * k + 12 * (t - 2)
                            tr[dst + 4 * k : dst + 4 * k + 4, :] = ref[first : first + 4, :]
                    else:
                        first = base + 48 * (t - 4)
                        tr[dst : dst + 16, :] = ref[first : first + 16, :]

    def prepare(send, section):
        for b in range(blocks):
            parts = split3(tr[b * ROWS : (b + 1) * ROWS, :])
            for s in range(3):
                t3[s * ROWS : (s + 1) * ROWS, b * LANES : (b + 1) * LANES] = parts[s]
        out = dot_nt(t3[...], oh[...])
        out = out[:ROWS] + out[ROWS : 2 * ROWS] + out[2 * ROWS :]
        for j in range(shared_blocks):
            block = jnp.concatenate(
                [out[:, j * LANES : (j + 1) * LANES], jnp.zeros((LANES - ROWS, LANES), F32)], axis=0
            )
            flipped = block.T
            for p in range(8):
                send[j * 8 + p, 0:16, :] = flipped[p * 16 : (p + 1) * 16, :]
        for side in range(2):
            first = (shared_blocks + side) * LANES
            rs[section, side] = out[:, first : first + LANES]

    def copies(send, receive, section):
        made = []
        for d in range(1, nd):
            peer = lax.rem(me + d, nd)
            made.append(
                pltpu.make_async_remote_copy(
                    src_ref=send.at[peer],
                    dst_ref=receive.at[me],
                    send_sem=send_sem.at[section, d],
                    recv_sem=recv_sem.at[section, d],
                    device_id={"dom": peer},
                    device_id_type=MESH,
                )
            )
        for side, target in ((0, down), (1, up)):
            made.append(
                pltpu.make_async_remote_copy(
                    src_ref=rs.at[section, side],
                    dst_ref=rr.at[section, 1 - side],
                    send_sem=rim_send_sem.at[section, side],
                    recv_sem=rim_recv_sem.at[section, 1 - side],
                    device_id={"group": target},
                    device_id_type=MESH,
                )
            )
        return made

    def waits(send, receive, section):
        for d in range(1, nd):
            source = lax.rem(me + nd - d, nd)
            pltpu.make_async_remote_copy(
                src_ref=send.at[lax.rem(me + d, nd)],
                dst_ref=receive.at[source],
                send_sem=send_sem.at[section, d],
                recv_sem=recv_sem.at[section, d],
                device_id={"dom": lax.rem(me + d, nd)},
                device_id_type=MESH,
            ).wait()
        for side, target in ((0, down), (1, up)):
            pltpu.make_async_remote_copy(
                src_ref=rs.at[section, side],
                dst_ref=rr.at[section, side],
                send_sem=rim_send_sem.at[section, side],
                recv_sem=rim_recv_sem.at[section, side],
                device_id={"group": target},
                device_id_type=MESH,
            ).wait()

    def gather_own(ob, carry):
        index = lk[ob]
        lane = index & (LANES - 1)
        where = index >> 7
        acc = [jnp.zeros((8, LANES), F32) for _ in range(10)]
        for sb in range(blocks):
            hit = where == sb
            for r in range(10):
                first = sb * ROWS + r * 8
                acc[r] = jnp.where(hit, pick_lanes(tr[first : first + 8, :], lane), acc[r])
        for r in range(10):
            nb[ob, r * 8 : r * 8 + 8, :] = acc[r]
        return carry

    def gather_arrived(ob, carry):
        index = lk[ob]
        lane = index & (LANES - 1)
        where = index >> 7
        for r in range(10):
            acc = nb[ob, r * 8 : r * 8 + 8, :]
            for sb in range(extra):
                acc = jnp.where(
                    where == blocks + sb, pick_lanes(ex[sb, r * 8 : r * 8 + 8, :], lane), acc
                )
            nb[ob, r * 8 : r * 8 + 8, :] = acc
        return carry

    def unpack(receive, section):
        for j in range(shared_blocks):
            block = jnp.concatenate([receive[j * 8 + p, 0:16, :] for p in range(8)], axis=0)
            ex[j] = block.T[:ROWS]
        for side in range(2):
            ex[shared_blocks + side] = rr[section, side]

    def volume(ref):
        for c in range(cols):
            lanes = slice(c * LANES, (c + 1) * LANES)
            for n in range(0, NODES, 16):
                rows = [ref[at(v, c) + n : at(v, c) + n + 16, :] for v in range(5)]
                _, vel, press = state_of(rows)
                for d in range(3):
                    flux = flux_of(rows, vel, press, d)
                    for v in range(5):
                        high, low = split2(flux[v])
                        fx[v, d * NODES + n : d * NODES + n + 16, lanes] = high
                        fx[v, (3 + d) * NODES + n : (3 + d) * NODES + n + 16, lanes] = low
        for v in range(5):
            out = jnp.dot(dmat[...], fx[v], preferred_element_type=F32)
            out = -(out[:NODES] + out[NODES:])
            for c in range(cols):
                td[at(v, c) : at(v, c) + NODES, :] = out[:, c * LANES : (c + 1) * LANES]

    def surface():
        for t in range(6):
            d = t // 2
            outward = 1.0 if t % 2 else -1.0
            for c in range(cols):
                b = t * cols + c
                inside = [tr[b * ROWS + v * 16 : b * ROWS + v * 16 + 16, :] for v in range(5)]
                outside = [nb[b, v * 16 : v * 16 + 16, :] for v in range(5)]
                inv_a, vel_a, press_a = state_of(inside)
                inv_b, vel_b, press_b = state_of(outside)
                lam = jnp.maximum(
                    jnp.abs(vel_a[d]) + jnp.sqrt(HEAT_RATIO * press_a * inv_a),
                    jnp.abs(vel_b[d]) + jnp.sqrt(HEAT_RATIO * press_b * inv_b),
                )
                lam = (0.5 * LIFT_FACTOR) * lam
                flux_a = flux_of(inside, vel_a, press_a, d)
                flux_b = flux_of(outside, vel_b, press_b, d)
                for v in range(5):
                    fix = lam * (outside[v] - inside[v]) - (0.5 * LIFT_FACTOR * outward) * (
                        flux_b[v] - flux_a[v]
                    )
                    base = at(v, c)
                    if t < 2:
                        place = pl.ds(base + 3 * t, 16, 4)
                        td[place, :] = td[place, :] + fix
                    elif t < 4:
                        for k in range(4):
                            first = base + 16 * k + 12 * (t - 2)
                            td[first : first + 4, :] = (
                                td[first : first + 4, :] + fix[4 * k : 4 * k + 4, :]
                            )
                    else:
                        first = base + 48 * (t - 4)
                        td[first : first + 16, :] = td[first : first + 16, :] + fix

    def finish(ref, second):
        for c in range(cols):
            lanes = slice(c * LANES, (c + 1) * LANES)
            for n in range(0, NODES, 16):
                rows = [ref[at(v, c) + n : at(v, c) + n + 16, :] for v in range(5)]
                rate = [td[at(v, c) + n : at(v, c) + n + 16, :] for v in range(5)]
                push = [src[k * NODES + n : k * NODES + n + 16, lanes] for k in range(3)]
                inverse = 1.0 / rows[0]
                work = (push[0] * rows[1] + push[1] * rows[2] + push[2] * rows[3]) * inverse
                rate = [
                    rate[0], rate[1] + push[0], rate[2] + push[1], rate[3] + push[2], rate[4] + work
                ]
                for v in range(5):
                    moved = rows[v] + TIME_STEP * rate[v]
                    if second:
                        o_tend[v, n : n + 16, lanes] = rate[v]
                        moved = 0.75 * q[at(v, c) + n : at(v, c) + n + 16, :] + 0.25 * moved
                    high, low = split2(moved)
                    xf[v, n : n + 16, lanes] = high
                    xf[v, NODES + n : NODES + n + 16, lanes] = low
        for v in range(5):
            out = jnp.dot(fmat[...], xf[v], preferred_element_type=F32)
            out = out[:NODES] + out[NODES:]
            if not second:
                for c in range(cols):
                    q1[at(v, c) : at(v, c) + NODES, :] = out[:, c * LANES : (c + 1) * LANES]
            elif v == 0:
                o_den[...] = out
            elif v == 4:
                o_ene[...] = out
            else:
                o_mom[v - 1] = out

    def pack_points():
        column = jnp.broadcast_to(rank[...].astype(F32), (LANES, LANES))
        across = column.T
        earlier = lax.broadcasted_iota(jnp.int32, (LANES, LANES), 1) < lax.broadcasted_iota(
            jnp.int32, (LANES, LANES), 0
        )
        place = jnp.sum(
            jnp.where((column == across) & earlier, 1.0, 0.0), axis=1, keepdims=True
        )
        target = column[:, 0:1] * float(LANES) + place
        slots = lax.broadcasted_iota(jnp.int32, (LANES, nd * LANES), 1).astype(F32)
        total = None
        for k in range(4):
            spread = jnp.where(target + float(k * CAP) == slots, 1.0, 0.0).astype(BF16)
            data = jnp.concatenate(
                [elem[k : k + 1, :].astype(F32)]
                + [off[x, k : k + 1, :] for x in range(3)]
                + [force[...], jnp.zeros((1, LANES), F32)],
                axis=0,
            )
            stacked = jnp.concatenate([part.astype(F32) for part in split3(data)], axis=0)
            out = jnp.dot(stacked.astype(BF16), spread, preferred_element_type=F32)
            total = out if total is None else total + out
        total = total[:8] + total[8:16] + total[16:]
        for a in range(nd):
            s1[a, 16:24, :] = total[:, a * LANES : (a + 1) * LANES]

    def spread_sources():
        n = lax.broadcasted_iota(jnp.int32, (NODES, LANES), 0)
        places = [n & 3, (n >> 2) & 3, n >> 4]
        coords = [
            jnp.where(
                p < 2,
                jnp.where(p == 0, float(nodes[0]), float(nodes[1])),
                jnp.where(p == 2, float(nodes[2]), float(nodes[3])),
            )
            for p in places
        ]
        element_ids = lax.broadcasted_iota(jnp.int32, (width, LANES), 0).astype(F32)
        for b in range(nd):
            lanes = slice(b * LANES, (b + 1) * LANES)
            tile = r1[b, 16:24, :]
            ohe[:, lanes] = jnp.where(element_ids == tile[0:1, :], 1.0, 0.0).astype(BF16)
            gap = [coords[x] - tile[1 + x : 2 + x, :] for x in range(3)]
            distance = gap[0] * gap[0] + gap[1] * gap[1] + gap[2] * gap[2]
            weight = jnp.exp(distance * (-1.0 / SPREAD_WIDTH))
            for x in range(3):
                high, low = split2(weight * tile[4 + x : 5 + x, :])
                ct[x * NODES : (x + 1) * NODES, lanes] = high
                ct[(3 + x) * NODES : (4 + x) * NODES, lanes] = low
        out = dot_nt(ct[...], ohe[...])
        src[...] = out[: 3 * NODES] + out[3 * NODES :]

    fill_traces(q)
    pack_points()
    prepare(s1, 0)
    pl.semaphore_wait(barrier, nd + 1)
    for copy in copies(s1, r1, 0):
        copy.start()
    r1[me] = s1[me]
    volume(q)
    lax.fori_loop(0, blocks, gather_own, 0)
    waits(s1, r1, 0)
    unpack(r1, 0)
    spread_sources()
    lax.fori_loop(0, blocks, gather_arrived, 0)
    surface()
    finish(q, False)

    fill_traces(q1)
    prepare(s2, 1)
    for copy in copies(s2, r2, 1):
        copy.start()
    r2[me] = s2[me]
    volume(q1)
    lax.fori_loop(0, blocks, gather_own, 0)
    waits(s2, r2, 1)
    unpack(r2, 1)
    lax.fori_loop(0, blocks, gather_arrived, 0)
    surface()
    finish(q1, True)


def body(density, momentum, energy, face_link, owner_rank, owner_element, offsets, forces):
    nd, ng = lax.axis_size("dom"), lax.axis_size("group")
    width = density.shape[1]
    cols = width // LANES
    blocks = 6 * cols
    extra = nd * (width // 32) // LANES + 2
    nodes, dcat, filt = basis_tables()
    vmem = pl.BlockSpec(memory_space=pltpu.VMEM)
    shape = jax.ShapeDtypeStruct
    return pl.pallas_call(
        functools.partial(kernel, nd, ng, nodes),
        out_shape=(
            shape((NODES, width), F32),
            shape((3, NODES, width), F32),
            shape((NODES, width), F32),
            shape((5, NODES, width), F32),
        ),
        in_specs=[vmem] * 10,
        out_specs=(vmem,) * 4,
        scratch_shapes=[
            pltpu.VMEM((5 * cols * NODES, LANES), F32),
            pltpu.VMEM((5 * cols * NODES, LANES), F32),
            pltpu.VMEM((5 * cols * NODES, LANES), F32),
            pltpu.VMEM((blocks * ROWS, LANES), F32),
            pltpu.VMEM((blocks, ROWS, LANES), F32),
            pltpu.VMEM((3 * ROWS, blocks * LANES), BF16),
            pltpu.VMEM((extra * LANES, blocks * LANES), BF16),
            pltpu.VMEM((blocks, 8, LANES), jnp.int32),
            pltpu.VMEM((5, 6 * NODES, width), BF16),
            pltpu.VMEM((5, 2 * NODES, width), BF16),
            pltpu.VMEM((extra, ROWS, LANES), F32),
            pltpu.VMEM((3 * NODES, width), F32),
            pltpu.VMEM((width, nd * LANES), BF16),
            pltpu.VMEM((6 * NODES, nd * LANES), BF16),
            pltpu.VMEM((nd, 24, LANES), F32),
            pltpu.VMEM((nd, 24, LANES), F32),
            pltpu.VMEM((nd, 16, LANES), F32),
            pltpu.VMEM((nd, 16, LANES), F32),
            pltpu.VMEM((2, 2, ROWS, LANES), F32),
            pltpu.VMEM((2, 2, ROWS, LANES), F32),
            pltpu.SemaphoreType.DMA((2, nd)),
            pltpu.SemaphoreType.DMA((2, nd)),
            pltpu.SemaphoreType.DMA((2, 2)),
            pltpu.SemaphoreType.DMA((2, 2)),
        ],
        compiler_params=pltpu.CompilerParams(
            collective_id=0, has_side_effects=True, vmem_limit_bytes=48 * 1024 * 1024
        ),
    )(
        density,
        momentum,
        energy,
        face_link.reshape(1, 6 * width),
        owner_rank,
        owner_element,
        offsets,
        forces,
        jnp.asarray(split_table(dcat)),
        jnp.asarray(split_table(filt)),
    )


def solution(mesh):
    element = P(None, ("group", "dom"))
    stacked = P(None, None, ("group", "dom"))
    return jax.shard_map(
        body,
        mesh=mesh,
        in_specs=(
            element,
            stacked,
            element,
            P("group", "dom", None),
            P(("group", "dom"), None),
            element,
            stacked,
            element,
        ),
        out_specs=(element, stacked, element, stacked),
        check_vma=False,
    )
```

profile of v0, /device:TPU:0, one launch (start us, length us, event | category | flops | bytes accessed | tf_op | source)
XLA Modules:
  0.0 41.1 jit_solution(10742684424048541894)
XLA Ops:
  0.6 0.0 copy-start.9
  0.6 0.6 %copy-done.9 = s32[128,1]{0,1:T(1,128)S(1)} copy-done((s32[128,1]{0,1:T(1,128)S(1)}, s32[128,1]{0,1:T(1,128)}, u32[]{:S(2)}) %copy-start.9) | copy-done | bytes 536
  1.3 0.0 copy-start.4
  1.3 0.0 copy-start.5
  1.3 0.0 copy-start.6
  1.3 0.0 copy-start.7
  1.3 0.0 copy-start.8
  1.3 0.1 copy.14.rank
  1.4 0.6 %copy-done.4 = bf16[128,128]{1,0:T(8,128)(2,1)S(1)} copy-done((bf16[128,128]{1,0:T(8,128)(2,1)S(1)}, bf16[128,128]{1,0:T(8,128)(2,1)}, u32[]{:S(2)}) %copy-start.4) | copy-done | bytes 32792
  2.0 0.0 copy-done.5
  2.0 0.0 copy-done.6
  2.1 0.0 copy-done.7
  2.1 0.0 copy-done.8
  2.1 0.0 copy-start
  2.1 1.0 %copy-done = f32[3,64,512]{2,1,0:T(8,128)S(1)} copy-done((f32[3,64,512]{2,1,0:T(8,128)S(1)}, f32[3,64,512]{2,1,0:T(8,128)}, u32[]{:S(2)}) %copy-start) | copy-done | bytes 393240
  3.1 0.0 copy-start.1
  3.1 0.9 %copy-done.1 = f32[64,512]{1,0:T(8,128)S(1)} copy-done((f32[64,512]{1,0:T(8,128)S(1)}, f32[64,512]{1,0:T(8,128)}, u32[]{:S(2)}) %copy-start.1) | copy-done | bytes 131096
  4.0 0.0 copy-start.2
  4.0 0.9 %copy-done.2 = f32[64,512]{1,0:T(8,128)S(1)} copy-done((f32[64,512]{1,0:T(8,128)S(1)}, f32[64,512]{1,0:T(8,128)}, u32[]{:S(2)}) %copy-start.2) | copy-done | bytes 131096
  4.9 0.0 copy-start.3
  4.9 0.9 %copy-done.3 = bf16[128,384]{1,0:T(8,128)(2,1)S(1)} copy-done((bf16[128,384]{1,0:T(8,128)(2,1)S(1)}, bf16[128,384]{1,0:T(8,128)(2,1)}, u32[]{:S(2)}) %copy-start.3) | copy-done | bytes 98328
  5.8 32.4 %shard_map.129 = (f32[64,512]{1,0:T(8,128)S(1)}, f32[3,64,512]{2,1,0:T(8,128)S(1)}, f32[64,512]{1,0:T(8,128)S(1)}, f32[5,64,512]{2,1,0:T(8,128)S(1)}) custom-call(f32[64,512]{1,0:T(8,128)S(1)} %copy-done.1, f32[3,64,512]{2,1,0:T(8,128)S(1)} %copy-done, f32[64,512]{1,0:T(8,128)S(1)} %copy-done.2, s32[1,3072]{1,0:T(1,128)S(1)} %bitcast.1, ...), custom_call_target="tpu_custom_call" | custom-call | tf_op jit(solution)/shard_map/pallas_call | solution.py:439
  38.2 0.7 %copy.19 = f32[64,512]{1,0:T(8,128)} copy(f32[64,512]{1,0:T(8,128)S(1)} %get-tuple-element.8) | data formatting | bytes 262144
  38.8 0.7 %copy.20 = f32[3,64,512]{2,1,0:T(8,128)} copy(f32[3,64,512]{2,1,0:T(8,128)S(1)} %get-tuple-element.9) | data formatting | bytes 786432
  39.6 0.7 %copy.21 = f32[64,512]{1,0:T(8,128)} copy(f32[64,512]{1,0:T(8,128)S(1)} %get-tuple-element.10) | data formatting | bytes 262144
  40.2 0.8 %copy.22 = f32[5,64,512]{2,1,0:T(8,128)} copy(f32[5,64,512]{2,1,0:T(8,128)S(1)} %get-tuple-element.11) | data formatting | bytes 1310720
Async XLA Ops:
  0.6 0.7 %copy-start.9 = (s32[128,1]{0,1:T(1,128)S(1)}, s32[128,1]{0,1:T(1,128)}, u32[]{:S(2)}) copy-start(s32[128,1]{0,1:T(1,128)} %param.14) | copy-start | bytes 1540
  1.3 0.8 %copy-start.4 = (bf16[128,128]{1,0:T(8,128)(2,1)S(1)}, bf16[128,128]{1,0:T(8,128)(2,1)}, u32[]{:S(2)}) copy-start(bf16[128,128]{1,0:T(8,128)(2,1)} %constant.5.clone.fmat) | copy-start | bytes 98308
  1.3 0.8 %copy-start.5 = (s32[1,1,3072]{2,1,0:T(1,128)S(1)}, s32[1,1,3072]{2,1,0:T(1,128)}, u32[]{:S(2)}) copy-start(s32[1,1,3072]{2,1,0:T(1,128)} %param.13) | copy-start | bytes 36868
  1.3 0.8 %copy-start.6 = (f32[3,4,128]{2,1,0:T(4,128)S(1)}, f32[3,4,128]{2,1,0:T(4,128)}, u32[]{:S(2)}) copy-start(f32[3,4,128]{2,1,0:T(4,128)} %off.1) | copy-start | bytes 18436
  1.3 0.8 %copy-start.7 = (s32[4,128]{1,0:T(4,128)S(1)}, s32[4,128]{1,0:T(4,128)}, u32[]{:S(2)}) copy-start(s32[4,128]{1,0:T(4,128)} %elem.1) | copy-start | bytes 6148
  1.3 0.8 %copy-start.8 = (f32[3,128]{1,0:T(4,128)S(1)}, f32[3,128]{1,0:T(4,128)}, u32[]{:S(2)}) copy-start(f32[3,128]{1,0:T(4,128)} %force.1) | copy-start | bytes 4612
  2.1 1.0 %copy-start = (f32[3,64,512]{2,1,0:T(8,128)S(1)}, f32[3,64,512]{2,1,0:T(8,128)}, u32[]{:S(2)}) copy-start(f32[3,64,512]{2,1,0:T(8,128)} %mom.1) | copy-start | bytes 1179652
  3.1 0.9 %copy-start.1 = (f32[64,512]{1,0:T(8,128)S(1)}, f32[64,512]{1,0:T(8,128)}, u32[]{:S(2)}) copy-start(f32[64,512]{1,0:T(8,128)} %den.1) | copy-start | bytes 393220
  4.0 0.9 %copy-start.2 = (f32[64,512]{1,0:T(8,128)S(1)}, f32[64,512]{1,0:T(8,128)}, u32[]{:S(2)}) copy-start(f32[64,512]{1,0:T(8,128)} %ene.1) | copy-start | bytes 393220
  4.9 0.9 %copy-start.3 = (bf16[128,384]{1,0:T(8,128)(2,1)S(1)}, bf16[128,384]{1,0:T(8,128)(2,1)}, u32[]{:S(2)}) copy-start(bf16[128,384]{1,0:T(8,128)(2,1)} %constant.4.clone.dmat) | copy-start | bytes 294916
where the time goes:
time: 41.4 us; the launch traced here: 41.1 us
  Pallas kernels  32.4 us (78%)
  local copies, waits for them, and re-layouts  7.99 us (19%)
  between operations  0.68 us (2%)
    pallas_call x1, Pallas kernels, body(): pl.pallas_call(functools.partial(kernel, nd, ng, nodes), out_shape=(shape...  32.4 us
    unnamed x25, local copies, waits for them, and re-layouts  7.99 us

commit v1 on v0

--- a/solution.py
+++ b/solution.py
@@ -105,7 +105,7 @@
     nd, ng, nodes,
     den, mom, ene, link, rank, elem, off, force, dmat, fmat,
     o_den, o_mom, o_ene, o_tend,
-    q, q1, td, tr, nb, t3, oh, lk, fx, xf, ex, src, ohe, ct,
+    q, q1, td, tr, nb, t3, oh, tall, got, index, index_sem, fx, xf, ex, src, ohe, ct,
     s1, r1, s2, r2, rs, rr, send_sem, recv_sem, rim_send_sem, rim_recv_sem,
 ):
     width = den.shape[1]
@@ -118,6 +118,8 @@
     group = lax.axis_index("group")
     up, down = lax.rem(group + 1, ng), lax.rem(group + ng - 1, ng)
 
+    fetch = pltpu.make_async_copy(link, index, index_sem)
+    fetch.start()
     barrier = pltpu.get_barrier_semaphore()
     for d in range(1, nd):
         pl.semaphore_signal(
@@ -139,7 +141,6 @@
     row_ids = lax.broadcasted_iota(jnp.int32, (extra * LANES, LANES), 0) + 6 * width
     for b in range(blocks):
         part = link[0:1, b * LANES : (b + 1) * LANES]
-        lk[b] = jnp.broadcast_to(part, (8, LANES))
         oh[:, b * LANES : (b + 1) * LANES] = jnp.where(row_ids == part, 1.0, 0.0).astype(BF16)
 
     def fill_traces(ref):
@@ -224,39 +225,39 @@
                 device_id_type=MESH,
             ).wait()
 
-    def gather_own(ob, carry):
-        index = lk[ob]
-        lane = index & (LANES - 1)
-        where = index >> 7
-        acc = [jnp.zeros((8, LANES), F32) for _ in range(10)]
-        for sb in range(blocks):
-            hit = where == sb
-            for r in range(10):
-                first = sb * ROWS + r * 8
-                acc[r] = jnp.where(hit, pick_lanes(tr[first : first + 8, :], lane), acc[r])
-        for r in range(10):
-            nb[ob, r * 8 : r * 8 + 8, :] = acc[r]
-        return carry
-
-    def gather_arrived(ob, carry):
-        index = lk[ob]
-        lane = index & (LANES - 1)
-        where = index >> 7
-        for r in range(10):
-            acc = nb[ob, r * 8 : r * 8 + 8, :]
-            for sb in range(extra):
-                acc = jnp.where(
-                    where == blocks + sb, pick_lanes(ex[sb, r * 8 : r * 8 + 8, :], lane), acc
-                )
-            nb[ob, r * 8 : r * 8 + 8, :] = acc
-        return carry
+    def turn_traces():
+        for b in range(blocks):
+            block = jnp.concatenate(
+                [tr[b * ROWS : (b + 1) * ROWS, :], jnp.zeros((LANES - ROWS, LANES), F32)], axis=0
+            )
+            tall[b * LANES : (b + 1) * LANES, :] = block.T
+
+    def gather_own():
+        def rows_of(ob, carry):
+            for r in range(LANES):
+                face = ob * LANES + r
+                got[pl.ds(face, 1), :] = tall[pl.ds(index[0, face], 1), :]
+            return carry
+
+        lax.fori_loop(0, blocks, rows_of, 0)
+        for b in range(blocks):
+            nb[b] = got[b * LANES : (b + 1) * LANES, :].T[:ROWS]
 
     def unpack(receive, section):
         for j in range(shared_blocks):
             block = jnp.concatenate([receive[j * 8 + p, 0:16, :] for p in range(8)], axis=0)
-            ex[j] = block.T[:ROWS]
+            ex[:, j * LANES : (j + 1) * LANES] = block.T[:ROWS]
         for side in range(2):
-            ex[shared_blocks + side] = rr[section, side]
+            first = (shared_blocks + side) * LANES
+            ex[:, first : first + LANES] = rr[section, side]
+
+    def gather_arrived():
+        parts = split2(ex[...])
+        stacked = jnp.concatenate(parts, axis=0)
+        out = jnp.dot(stacked, oh[...], preferred_element_type=F32)
+        for b in range(blocks):
+            lanes = slice(b * LANES, (b + 1) * LANES)
+            nb[b] = nb[b] + (out[:ROWS, lanes] + out[ROWS:, lanes])
 
     def volume(ref):
         for c in range(cols):
@@ -397,6 +398,8 @@
         out = dot_nt(ct[...], ohe[...])
         src[...] = out[: 3 * NODES] + out[3 * NODES :]
 
+    tall[6 * width :, :] = jnp.zeros((extra * LANES, LANES), F32)
+    fetch.wait()
     fill_traces(q)
     pack_points()
     prepare(s1, 0)
@@ -404,12 +407,13 @@
     for copy in copies(s1, r1, 0):
         copy.start()
     r1[me] = s1[me]
+    turn_traces()
     volume(q)
-    lax.fori_loop(0, blocks, gather_own, 0)
+    gather_own()
     waits(s1, r1, 0)
     unpack(r1, 0)
     spread_sources()
-    lax.fori_loop(0, blocks, gather_arrived, 0)
+    gather_arrived()
     surface()
     finish(q, False)
 
@@ -418,11 +422,12 @@
     for copy in copies(s2, r2, 1):
         copy.start()
     r2[me] = s2[me]
+    turn_traces()
     volume(q1)
-    lax.fori_loop(0, blocks, gather_own, 0)
+    gather_own()
     waits(s2, r2, 1)
     unpack(r2, 1)
-    lax.fori_loop(0, blocks, gather_arrived, 0)
+    gather_arrived()
     surface()
     finish(q1, True)
 
@@ -454,10 +459,13 @@
             pltpu.VMEM((blocks, ROWS, LANES), F32),
             pltpu.VMEM((3 * ROWS, blocks * LANES), BF16),
             pltpu.VMEM((extra * LANES, blocks * LANES), BF16),
-            pltpu.VMEM((blocks, 8, LANES), jnp.int32),
+            pltpu.VMEM(((blocks + extra) * LANES, LANES), F32),
+            pltpu.VMEM((blocks * LANES, LANES), F32),
+            pltpu.SMEM((1, 6 * width), jnp.int32),
+            pltpu.SemaphoreType.DMA,
             pltpu.VMEM((5, 6 * NODES, width), BF16),
             pltpu.VMEM((5, 2 * NODES, width), BF16),
-            pltpu.VMEM((extra, ROWS, LANES), F32),
+            pltpu.VMEM((ROWS, extra * LANES), F32),
             pltpu.VMEM((3 * NODES, width), F32),
             pltpu.VMEM((width, nd * LANES), BF16),
             pltpu.VMEM((6 * NODES, nd * LANES), BF16),

time: 41.4 us -> 28.5 us (0.69)
  Pallas kernels: 32.4 us -> 19.6 us
    pallas_call x1, Pallas kernels: 32.4 us -> 19.6 us  [body(): pl.pallas_call(functools.partial(kernel, nd, ng, nodes), out_shape=(shape...]
where the time goes in v1:
time: 28.5 us; the launch traced here: 28.2 us
  Pallas kernels  19.6 us (69%)
  local copies, waits for them, and re-layouts  7.99 us (28%)
  between operations  0.68 us (2%)
    pallas_call x1, Pallas kernels, body(): pl.pallas_call(functools.partial(kernel, nd, ng, nodes), out_shape=(shape...  19.6 us
    unnamed x25, local copies, waits for them, and re-layouts  7.99 us

profile of v1, /device:TPU:0, one launch (start us, length us, event | category | flops | bytes accessed | tf_op | source)
XLA Modules:
  0.0 28.2 jit_solution(17877562801354439353)
XLA Ops:
  0.6 0.0 copy-start.9
  0.6 0.6 %copy-done.9 = s32[128,1]{0,1:T(1,128)S(1)} copy-done((s32[128,1]{0,1:T(1,128)S(1)}, s32[128,1]{0,1:T(1,128)}, u32[]{:S(2)}) %copy-start.9) | copy-done | bytes 536
  1.3 0.0 copy-start.4
  1.3 0.0 copy-start.5
  1.3 0.0 copy-start.6
  1.3 0.0 copy-start.7
  1.3 0.0 copy-start.8
  1.3 0.1 copy.14.rank
  1.4 0.6 %copy-done.4 = bf16[128,128]{1,0:T(8,128)(2,1)S(1)} copy-done((bf16[128,128]{1,0:T(8,128)(2,1)S(1)}, bf16[128,128]{1,0:T(8,128)(2,1)}, u32[]{:S(2)}) %copy-start.4) | copy-done | bytes 32792
  2.0 0.0 copy-done.5
  2.0 0.0 copy-done.6
  2.1 0.0 copy-done.7
  2.1 0.0 copy-done.8
  2.1 0.0 copy-start
  2.1 1.0 %copy-done = f32[3,64,512]{2,1,0:T(8,128)S(1)} copy-done((f32[3,64,512]{2,1,0:T(8,128)S(1)}, f32[3,64,512]{2,1,0:T(8,128)}, u32[]{:S(2)}) %copy-start) | copy-done | bytes 393240
  3.1 0.0 copy-start.1
  3.1 0.9 %copy-done.1 = f32[64,512]{1,0:T(8,128)S(1)} copy-done((f32[64,512]{1,0:T(8,128)S(1)}, f32[64,512]{1,0:T(8,128)}, u32[]{:S(2)}) %copy-start.1) | copy-done | bytes 131096
  4.0 0.0 copy-start.2
  4.0 0.9 %copy-done.2 = f32[64,512]{1,0:T(8,128)S(1)} copy-done((f32[64,512]{1,0:T(8,128)S(1)}, f32[64,512]{1,0:T(8,128)}, u32[]{:S(2)}) %copy-start.2) | copy-done | bytes 131096
  4.9 0.0 copy-start.3
  4.9 0.9 %copy-done.3 = bf16[128,384]{1,0:T(8,128)(2,1)S(1)} copy-done((bf16[128,384]{1,0:T(8,128)(2,1)S(1)}, bf16[128,384]{1,0:T(8,128)(2,1)}, u32[]{:S(2)}) %copy-start.3) | copy-done | bytes 98328
  5.8 19.6 %shard_map.129 = (f32[64,512]{1,0:T(8,128)S(1)}, f32[3,64,512]{2,1,0:T(8,128)S(1)}, f32[64,512]{1,0:T(8,128)S(1)}, f32[5,64,512]{2,1,0:T(8,128)S(1)}) custom-call(f32[64,512]{1,0:T(8,128)S(1)} %copy-done.1, f32[3,64,512]{2,1,0:T(8,128)S(1)} %copy-done, f32[64,512]{1,0:T(8,128)S(1)} %copy-done.2, s32[1,3072]{1,0:T(1,128)S(1)} %bitcast.1, ...), custom_call_target="tpu_custom_call" | custom-call | tf_op jit(solution)/shard_map/pallas_call | solution.py:444
  25.3 0.7 %copy.19 = f32[64,512]{1,0:T(8,128)} copy(f32[64,512]{1,0:T(8,128)S(1)} %get-tuple-element.8) | data formatting | bytes 262144
  26.0 0.7 %copy.20 = f32[3,64,512]{2,1,0:T(8,128)} copy(f32[3,64,512]{2,1,0:T(8,128)S(1)} %get-tuple-element.9) | data formatting | bytes 786432
  26.8 0.7 %copy.21 = f32[64,512]{1,0:T(8,128)} copy(f32[64,512]{1,0:T(8,128)S(1)} %get-tuple-element.10) | data formatting | bytes 262144
  27.4 0.8 %copy.22 = f32[5,64,512]{2,1,0:T(8,128)} copy(f32[5,64,512]{2,1,0:T(8,128)S(1)} %get-tuple-element.11) | data formatting | bytes 1310720
Async XLA Ops:
  0.6 0.7 %copy-start.9 = (s32[128,1]{0,1:T(1,128)S(1)}, s32[128,1]{0,1:T(1,128)}, u32[]{:S(2)}) copy-start(s32[128,1]{0,1:T(1,128)} %param.14) | copy-start | bytes 1540
  1.3 0.8 %copy-start.4 = (bf16[128,128]{1,0:T(8,128)(2,1)S(1)}, bf16[128,128]{1,0:T(8,128)(2,1)}, u32[]{:S(2)}) copy-start(bf16[128,128]{1,0:T(8,128)(2,1)} %constant.5.clone.fmat) | copy-start | bytes 98308
  1.3 0.8 %copy-start.5 = (s32[1,1,3072]{2,1,0:T(1,128)S(1)}, s32[1,1,3072]{2,1,0:T(1,128)}, u32[]{:S(2)}) copy-start(s32[1,1,3072]{2,1,0:T(1,128)} %param.13) | copy-start | bytes 36868
  1.3 0.8 %copy-start.6 = (f32[3,4,128]{2,1,0:T(4,128)S(1)}, f32[3,4,128]{2,1,0:T(4,128)}, u32[]{:S(2)}) copy-start(f32[3,4,128]{2,1,0:T(4,128)} %off.1) | copy-start | bytes 18436
  1.3 0.8 %copy-start.7 = (s32[4,128]{1,0:T(4,128)S(1)}, s32[4,128]{1,0:T(4,128)}, u32[]{:S(2)}) copy-start(s32[4,128]{1,0:T(4,128)} %elem.1) | copy-start | bytes 6148
  1.3 0.8 %copy-start.8 = (f32[3,128]{1,0:T(4,128)S(1)}, f32[3,128]{1,0:T(4,128)}, u32[]{:S(2)}) copy-start(f32[3,128]{1,0:T(4,128)} %force.1) | copy-start | bytes 4612
  2.1 1.0 %copy-start = (f32[3,64,512]{2,1,0:T(8,128)S(1)}, f32[3,64,512]{2,1,0:T(8,128)}, u32[]{:S(2)}) copy-start(f32[3,64,512]{2,1,0:T(8,128)} %mom.1) | copy-start | bytes 1179652
  3.1 0.9 %copy-start.1 = (f32[64,512]{1,0:T(8,128)S(1)}, f32[64,512]{1,0:T(8,128)}, u32[]{:S(2)}) copy-start(f32[64,512]{1,0:T(8,128)} %den.1) | copy-start | bytes 393220
  4.0 0.9 %copy-start.2 = (f32[64,512]{1,0:T(8,128)S(1)}, f32[64,512]{1,0:T(8,128)}, u32[]{:S(2)}) copy-start(f32[64,512]{1,0:T(8,128)} %ene.1) | copy-start | bytes 393220
  4.9 0.9 %copy-start.3 = (bf16[128,384]{1,0:T(8,128)(2,1)S(1)}, bf16[128,384]{1,0:T(8,128)(2,1)}, u32[]{:S(2)}) copy-start(bf16[128,384]{1,0:T(8,128)(2,1)} %constant.4.clone.dmat) | copy-start | bytes 294916

commit v2 on v1

--- a/solution.py
+++ b/solution.py
@@ -101,13 +101,38 @@
     return out
 
 
+def place_kernel(den, mom, ene, tend, o_den, o_mom, o_ene, o_tend, sem):
+    pairs = [(tend.at[v], o_tend.at[v]) for v in range(5)]
+    pairs += [(mom.at[v], o_mom.at[v]) for v in range(3)] + [(den, o_den), (ene, o_ene)]
+    moves = [
+        pltpu.make_async_copy(source, target, sem.at[i])
+        for i, (source, target) in enumerate(pairs)
+    ]
+    for move in moves:
+        move.start()
+    for move in moves:
+        move.wait()
+
+
 def kernel(
     nd, ng, nodes,
-    den, mom, ene, link, rank, elem, off, force, dmat, fmat,
-    o_den, o_mom, o_ene, o_tend,
+    den_in, mom_in, ene_in, link_in, rank_in, elem_in, off_in, force_in, dmat_in, fmat_in,
+    to_den, to_mom, to_ene, to_tend,
+    den, mom, ene, link, rank, elem, off, force, dmat, fmat, load_sem,
+    o_den, o_mom, o_ene, o_tend, store_sem,
     q, q1, td, tr, nb, t3, oh, tall, got, index, index_sem, fx, xf, ex, src, ohe, ct,
     s1, r1, s2, r2, rs, rr, send_sem, recv_sem, rim_send_sem, rim_recv_sem,
 ):
+    pairs = (
+        (link_in, link), (den_in, den), (mom_in, mom), (ene_in, ene), (rank_in, rank),
+        (elem_in, elem), (off_in, off), (force_in, force), (dmat_in, dmat), (fmat_in, fmat),
+    )
+    loads = [
+        pltpu.make_async_copy(source, target, load_sem.at[i])
+        for i, (source, target) in enumerate(pairs)
+    ]
+    for load in loads:
+        load.start()
     width = den.shape[1]
     cols = width // LANES
     blocks = 6 * cols
@@ -118,7 +143,7 @@
     group = lax.axis_index("group")
     up, down = lax.rem(group + 1, ng), lax.rem(group + ng - 1, ng)
 
-    fetch = pltpu.make_async_copy(link, index, index_sem)
+    fetch = pltpu.make_async_copy(link_in, index, index_sem)
     fetch.start()
     barrier = pltpu.get_barrier_semaphore()
     for d in range(1, nd):
@@ -131,17 +156,20 @@
     def at(v, c):
         return (v * cols + c) * NODES
 
+    loads[0].wait()
+    row_ids = lax.broadcasted_iota(jnp.int32, (extra * LANES, LANES), 0) + 6 * width
+    for b in range(blocks):
+        part = link[0:1, b * LANES : (b + 1) * LANES]
+        oh[:, b * LANES : (b + 1) * LANES] = jnp.where(row_ids == part, 1.0, 0.0).astype(BF16)
+
+    for load in loads[1:]:
+        load.wait()
     for c in range(cols):
         lanes = slice(c * LANES, (c + 1) * LANES)
         q[at(0, c) : at(0, c) + NODES, :] = den[:, lanes]
         for v in range(3):
             q[at(1 + v, c) : at(1 + v, c) + NODES, :] = mom[v, :, lanes]
         q[at(4, c) : at(4, c) + NODES, :] = ene[:, lanes]
-
-    row_ids = lax.broadcasted_iota(jnp.int32, (extra * LANES, LANES), 0) + 6 * width
-    for b in range(blocks):
-        part = link[0:1, b * LANES : (b + 1) * LANES]
-        oh[:, b * LANES : (b + 1) * LANES] = jnp.where(row_ids == part, 1.0, 0.0).astype(BF16)
 
     def fill_traces(ref):
         for c in range(cols):
@@ -272,7 +300,7 @@
                         fx[v, d * NODES + n : d * NODES + n + 16, lanes] = high
                         fx[v, (3 + d) * NODES + n : (3 + d) * NODES + n + 16, lanes] = low
         for v in range(5):
-            out = jnp.dot(dmat[...], fx[v], preferred_element_type=F32)
+            out = jnp.dot(dmat[...].astype(BF16), fx[v], preferred_element_type=F32)
             out = -(out[:NODES] + out[NODES:])
             for c in range(cols):
                 td[at(v, c) : at(v, c) + NODES, :] = out[:, c * LANES : (c + 1) * LANES]
@@ -332,8 +360,16 @@
                     high, low = split2(moved)
                     xf[v, n : n + 16, lanes] = high
                     xf[v, NODES + n : NODES + n + 16, lanes] = low
+        stores = []
+        if second:
+            stores.append(pltpu.make_async_copy(o_tend, to_tend, store_sem.at[5]))
+            stores[0].start()
+        targets = [
+            (o_den, to_den), (o_mom.at[0], to_mom.at[0]), (o_mom.at[1], to_mom.at[1]),
+            (o_mom.at[2], to_mom.at[2]), (o_ene, to_ene),
+        ]
         for v in range(5):
-            out = jnp.dot(fmat[...], xf[v], preferred_element_type=F32)
+            out = jnp.dot(fmat[...].astype(BF16), xf[v], preferred_element_type=F32)
             out = out[:NODES] + out[NODES:]
             if not second:
                 for c in range(cols):
@@ -344,10 +380,15 @@
                 o_ene[...] = out
             else:
                 o_mom[v - 1] = out
+            if second:
+                stores.append(pltpu.make_async_copy(*targets[v], store_sem.at[v]))
+                stores[-1].start()
+        for store in stores:
+            store.wait()
 
     def pack_points():
-        column = jnp.broadcast_to(rank[...].astype(F32), (LANES, LANES))
-        across = column.T
+        across = jnp.broadcast_to(rank[...].astype(F32), (LANES, LANES))
+        column = across.T
         earlier = lax.broadcasted_iota(jnp.int32, (LANES, LANES), 1) < lax.broadcasted_iota(
             jnp.int32, (LANES, LANES), 0
         )
@@ -439,19 +480,37 @@
     blocks = 6 * cols
     extra = nd * (width // 32) // LANES + 2
     nodes, dcat, filt = basis_tables()
-    vmem = pl.BlockSpec(memory_space=pltpu.VMEM)
+    points = owner_rank.shape[0]
+    hbm = pl.BlockSpec(memory_space=pltpu.HBM)
     shape = jax.ShapeDtypeStruct
-    return pl.pallas_call(
+    results = (
+        shape((NODES, width), F32),
+        shape((3, NODES, width), F32),
+        shape((NODES, width), F32),
+        shape((5, NODES, width), F32),
+    )
+    held = pl.pallas_call(
         functools.partial(kernel, nd, ng, nodes),
-        out_shape=(
-            shape((NODES, width), F32),
-            shape((3, NODES, width), F32),
-            shape((NODES, width), F32),
-            shape((5, NODES, width), F32),
-        ),
-        in_specs=[vmem] * 10,
-        out_specs=(vmem,) * 4,
+        out_shape=results,
+        in_specs=[hbm] * 10,
+        out_specs=(hbm,) * 4,
         scratch_shapes=[
+            pltpu.VMEM((NODES, width), F32),
+            pltpu.VMEM((3, NODES, width), F32),
+            pltpu.VMEM((NODES, width), F32),
+            pltpu.VMEM((1, 6 * width), jnp.int32),
+            pltpu.VMEM((1, points), jnp.int32),
+            pltpu.VMEM((4, points), jnp.int32),
+            pltpu.VMEM((3, 4, points), F32),
+            pltpu.VMEM((3, points), F32),
+            pltpu.VMEM((2 * NODES, 6 * NODES), F32),
+            pltpu.VMEM((2 * NODES, 2 * NODES), F32),
+            pltpu.SemaphoreType.DMA((10,)),
+            pltpu.VMEM((NODES, width), F32),
+            pltpu.VMEM((3, NODES, width), F32),
+            pltpu.VMEM((NODES, width), F32),
+            pltpu.VMEM((5, NODES, width), F32),
+            pltpu.SemaphoreType.DMA((6,)),
             pltpu.VMEM((5 * cols * NODES, LANES), F32),
             pltpu.VMEM((5 * cols * NODES, LANES), F32),
             pltpu.VMEM((5 * cols * NODES, LANES), F32),
@@ -481,20 +540,28 @@
             pltpu.SemaphoreType.DMA((2, 2)),
         ],
         compiler_params=pltpu.CompilerParams(
-            collective_id=0, has_side_effects=True, vmem_limit_bytes=48 * 1024 * 1024
+            collective_id=0, has_side_effects=True, vmem_limit_bytes=60 * 1024 * 1024
         ),
     )(
         density,
         momentum,
         energy,
         face_link.reshape(1, 6 * width),
-        owner_rank,
+        owner_rank.reshape(1, points),
         owner_element,
         offsets,
         forces,
-        jnp.asarray(split_table(dcat)),
-        jnp.asarray(split_table(filt)),
-    )
+        jnp.asarray(split_table(dcat).astype(np.float32)),
+        jnp.asarray(split_table(filt).astype(np.float32)),
+    )
+    return pl.pallas_call(
+        place_kernel,
+        out_shape=results,
+        in_specs=[hbm] * 4,
+        out_specs=(hbm,) * 4,
+        scratch_shapes=[pltpu.SemaphoreType.DMA((10,))],
+        compiler_params=pltpu.CompilerParams(vmem_limit_bytes=60 * 1024 * 1024),
+    )(*held)
 
 
 def solution(mesh):

time: 28.5 us -> 63.1 us (2.21)
  Pallas kernels: 19.6 us -> 62.2 us
  local copies, waits for them, and re-layouts: 7.99 us -> 0 us
    pallas_call x1 -> x2, Pallas kernels: 19.6 us -> 62.2 us  [the longest x1 40.9 us: body(): pl.pallas_call(place_kernel, out_shape=results, in_specs=[hbm] * 4, out_s...]
    unnamed x25 -> x0, local copies, waits for them, and re-layouts: 7.99 us -> none
where the time goes in v2:
time: 63.1 us; the launch traced here: 62.8 us
  Pallas kernels  62.2 us (99%)
  between operations  0.64 us (1%)
    pallas_call x1, Pallas kernels, body(): pl.pallas_call(place_kernel, out_shape=results, in_specs=[hbm] * 4, out_s...  40.9 us
    pallas_call x1, Pallas kernels, body(): pl.pallas_call(functools.partial(kernel, nd, ng, nodes), out_shape=result...  21.3 us

profile of v2, /device:TPU:0, one launch (start us, length us, event | category | flops | bytes accessed | tf_op | source)
XLA Modules:
  0.0 62.8 jit_solution(9104672292072340148)
XLA Ops:
  0.6 21.3 %shard_map.129 = (f32[64,512]{1,0:T(8,128)}, f32[3,64,512]{2,1,0:T(8,128)}, f32[64,512]{1,0:T(8,128)}, f32[5,64,512]{2,1,0:T(8,128)}) custom-call(f32[64,512]{1,0:T(8,128)} %den_in.1, f32[3,64,512]{2,1,0:T(8,128)} %mom_in.1, f32[64,512]{1,0:T(8,128)} %ene_in.1, s32[1,3072]{1,0:T(1,128)} %bitcast.2, s32[1,128]{1,0:T(1,128)} %bitcast.3, s32[4,128]{1,0:T(4,128)} %elem_in.1, ...), custom_call_target="tpu_custom_call" | custom-call | tf_op jit(solution)/shard_map/pallas_call | solution.py:492
  21.9 40.9 %shard_map.130 = (f32[64,512]{1,0:T(8,128)}, f32[3,64,512]{2,1,0:T(8,128)}, f32[64,512]{1,0:T(8,128)}, f32[5,64,512]{2,1,0:T(8,128)}) custom-call(f32[64,512]{1,0:T(8,128)} %get-tuple-element.8.den, f32[3,64,512]{2,1,0:T(8,128)} %get-tuple-element.9.mom, f32[64,512]{1,0:T(8,128)} %get-tuple-element.10.ene, f32[5,64,512]{2,1,0:T(8,128)} %get-tuple-element.11.tend), custom_call_target="tpu_custom_call" | custom-call | tf_op jit(solution)/shard_map/pallas_call | solution.py:557

commit v3 on v2

--- a/solution.py
+++ b/solution.py
@@ -101,17 +101,22 @@
     return out
 
 
-def place_kernel(den, mom, ene, tend, o_den, o_mom, o_ene, o_tend, sem):
+def place_kernel(den, mom, ene, tend, o_den, o_mom, o_ene, o_tend, held, load_sem, store_sem):
     pairs = [(tend.at[v], o_tend.at[v]) for v in range(5)]
     pairs += [(mom.at[v], o_mom.at[v]) for v in range(3)] + [(den, o_den), (ene, o_ene)]
-    moves = [
-        pltpu.make_async_copy(source, target, sem.at[i])
-        for i, (source, target) in enumerate(pairs)
+    loads = [
+        pltpu.make_async_copy(pair[0], held.at[i], load_sem.at[i]) for i, pair in enumerate(pairs)
     ]
-    for move in moves:
-        move.start()
-    for move in moves:
-        move.wait()
+    stores = [
+        pltpu.make_async_copy(held.at[i], pair[1], store_sem.at[i]) for i, pair in enumerate(pairs)
+    ]
+    for load in loads:
+        load.start()
+    for load, store in zip(loads, stores):
+        load.wait()
+        store.start()
+    for store in stores:
+        store.wait()
 
 
 def kernel(
@@ -559,7 +564,11 @@
         out_shape=results,
         in_specs=[hbm] * 4,
         out_specs=(hbm,) * 4,
-        scratch_shapes=[pltpu.SemaphoreType.DMA((10,))],
+        scratch_shapes=[
+            pltpu.VMEM((10, NODES, width), F32),
+            pltpu.SemaphoreType.DMA((10,)),
+            pltpu.SemaphoreType.DMA((10,)),
+        ],
         compiler_params=pltpu.CompilerParams(vmem_limit_bytes=60 * 1024 * 1024),
     )(*held)
 

time: 63.1 us -> 24.4 us (0.39)
  Pallas kernels: 62.2 us -> 23.5 us
    pallas_call x1, Pallas kernels: 40.9 us -> 2.21 us  [body(): pl.pallas_call(place_kernel, out_shape=results, in_specs=[hbm] * 4, out_s...]
where the time goes in v3:
time: 24.4 us; the launch traced here: 24.2 us
  Pallas kernels  23.5 us (96%)
  between operations  0.64 us (3%)
    pallas_call x1, Pallas kernels, body(): pl.pallas_call(functools.partial(kernel, nd, ng, nodes), out_shape=result...  21.3 us
    pallas_call x1, Pallas kernels, body(): pl.pallas_call(place_kernel, out_shape=results, in_specs=[hbm] * 4, out_s...  2.21 us

profile of v3, /device:TPU:0, one launch (start us, length us, event | category | flops | bytes accessed | tf_op | source)
XLA Modules:
  0.0 24.2 jit_solution(11316046091673878851)
XLA Ops:
  0.6 21.3 %shard_map.129 = (f32[64,512]{1,0:T(8,128)}, f32[3,64,512]{2,1,0:T(8,128)}, f32[64,512]{1,0:T(8,128)}, f32[5,64,512]{2,1,0:T(8,128)}) custom-call(f32[64,512]{1,0:T(8,128)} %den_in.1, f32[3,64,512]{2,1,0:T(8,128)} %mom_in.1, f32[64,512]{1,0:T(8,128)} %ene_in.1, s32[1,3072]{1,0:T(1,128)} %bitcast.2, s32[1,128]{1,0:T(1,128)} %bitcast.3, s32[4,128]{1,0:T(4,128)} %elem_in.1, ...), custom_call_target="tpu_custom_call" | custom-call | tf_op jit(solution)/shard_map/pallas_call | solution.py:497
  21.9 2.2 %shard_map.130 = (f32[64,512]{1,0:T(8,128)}, f32[3,64,512]{2,1,0:T(8,128)}, f32[64,512]{1,0:T(8,128)}, f32[5,64,512]{2,1,0:T(8,128)}) custom-call(f32[64,512]{1,0:T(8,128)} %get-tuple-element.8.den, f32[3,64,512]{2,1,0:T(8,128)} %get-tuple-element.9.mom, f32[64,512]{1,0:T(8,128)} %get-tuple-element.10.ene, f32[5,64,512]{2,1,0:T(8,128)} %get-tuple-element.11.tend), custom_call_target="tpu_custom_call" | custom-call | tf_op jit(solution)/shard_map/pallas_call | solution.py:562
